TPU v7x, 512 devices: a whole 4x8x8 slice. The times are simulated.
512 devices in a mesh: gx: 32 (over z_hi, y), gy: 4 (over z_lo, core), pa: 4 (over x).
Axes of the slice: x: 4, y: 8, z: 8 (z_hi: 4, z_lo: 2; z = z_hi * 2 + z_lo), core: 2. Of those that a mesh axis runs over, the one named last changes fastest.
Arguments:
- latents: bfloat16 [512, 128, 768], P(('gx', 'pa'), 'gy'), may hold values from -6 to 6
- noise: bfloat16 [2, 512, 128, 768], P(None, ('gx', 'pa'), 'gy'), may hold values from -6 to 6
- proc_gain: float32 [768], replicated, may hold values from 0.1 to 1.9
- w_qkv: bfloat16 [768, 2304], P(('gx', 'pa')), may hold values from -0.21875 to 0.21875
- w_out: bfloat16 [768, 768], P(('gx', 'pa')), may hold values from -0.21875 to 0.21875
- w_query: bfloat16 [128, 768], P(('gx', 'pa')), may hold values from -0.5 to 0.5
- w_head: bfloat16 [768, 3], P(('gx', 'pa')), may hold values from -0.21875 to 0.21875
- probe_cell: int32 [524288], P(('gx', 'gy', 'pa')), may hold values from 0 to 127
- probe_offset: float32 [2, 524288], P(None, ('gx', 'gy', 'pa')), may hold values from 0 to 1
- probe_count: int32 [512], P(('gx', 'gy', 'pa')), may hold values from 128 to 1024, as said below
Outputs:
- latent_out: bfloat16 [512, 128, 768], P(('gx', 'pa'), 'gy')
- probe_values: float32 [3, 524288], P(None, ('gx', 'gy', 'pa'))
Inputs may be any that keep to these rules, and one draw needn't show every extreme that they name: `probe_cell`: a cell of the device's own 4 x 32 block, numbered row by row. `probe_count`: slots below the count hold probes, the others are empty; in every draw one device has all 1024 slots live.
All inputs are finite; a program needn't handle non-finite values.
Results may differ from a plain program's by a relative error of at most 0.02.
Values may be sent and summed in bfloat16 or wider, within the bound.
No kernel may reach another device: no remote copies, remote signals or barrier semaphores. Data moves between devices by JAX's collectives and lax.ppermute only.
A program may use at most 64 MiB of HBM per device.

v0:
```python
import math
import jax
import jax.numpy as jnp
from jax import lax
from jax.sharding import PartitionSpec as P

HEADS = 12
FQ = 128
CH = 3
RAD = 3
STEPS = 2
EPS = 1e-06
NOISE_COEF = 0.3


def extended(block, sides, width):
    for axis, dim in sides:
        count = lax.axis_size(axis)
        forward = [(i, i + 1) for i in range(count - 1)]
        forward.append((count - 1, 0))
        backward = [(target, source) for source, target in forward]
        low = lax.ppermute(
            lax.slice_in_dim(block, block.shape[dim] - width, None, axis=dim), axis, forward
        )
        high = lax.ppermute(lax.slice_in_dim(block, 0, width, axis=dim), axis, backward)
        block = jnp.concatenate([low, block, high], axis=dim)
    return block


def normalize(tokens, gain_vec):
    values = tokens.astype(jnp.float32)
    factor = lax.rsqrt(jnp.mean(values * values, axis=-1, keepdims=True) + EPS)
    return (values * factor * gain_vec).astype(jnp.bfloat16)


def project(tokens, weight):
    leading = tokens.shape[:-1]
    flat_rows = tokens.reshape(-1, tokens.shape[-1])
    result = jnp.dot(flat_rows, weight, preferred_element_type=jnp.float32).astype(jnp.bfloat16)
    return result.reshape(leading + (weight.shape[1],))


def extend(latent_field):
    return extended(latent_field, ((("gx", "pa"), 0), ("gy", 1)), RAD)


def head_table(model_width):
    head_size = model_width // HEADS
    owner = jnp.arange(model_width, dtype=jnp.int32) // head_size
    return (owner[None, :] == jnp.arange(HEADS, dtype=jnp.int32)[:, None]).astype(jnp.float32)


def head_sums(table, product):
    return lax.dot_general(
        table,
        product,
        (((1,), (1,)), ((), ())),
        precision=lax.Precision.HIGHEST,
        preferred_element_type=jnp.float32,
    )


def head_spread(weight_rows, table_low):
    return lax.dot_general(
        weight_rows, table_low, (((0,), (0,)), ((), ())), preferred_element_type=jnp.float32
    )


def neighbour_attention(queries, key_values, row_count, col_count):
    model_width = queries.shape[-1]
    head_size = model_width // HEADS
    window_span = 2 * RAD + 1
    table = head_table(model_width)
    table_low = table.astype(jnp.bfloat16)
    query_flat = queries.reshape(-1, model_width).astype(jnp.float32)
    score_list = []
    for row_step in range(window_span):
        for col_step in range(window_span):
            key_flat = key_values[
                row_step : row_step + row_count, col_step : col_step + col_count, :model_width
            ].reshape(-1, model_width)
            score_list.append(head_sums(table, query_flat * key_flat.astype(jnp.float32)))
    scores = jnp.stack(score_list) / math.sqrt(head_size)
    weights = jax.nn.softmax(scores, axis=0).astype(jnp.bfloat16)
    summed = jnp.zeros((row_count * col_count, model_width), jnp.float32)
    for row_step in range(window_span):
        for col_step in range(window_span):
            value_flat = key_values[
                row_step : row_step + row_count, col_step : col_step + col_count, model_width:
            ].reshape(-1, model_width)
            spread = head_spread(weights[row_step * window_span + col_step], table_low)
            summed = summed + spread * value_flat.astype(jnp.float32)
    return summed.reshape(row_count, col_count, model_width).astype(jnp.bfloat16)


def decode_block(context, offsets, query_weight, head_weight):
    model_width = context.shape[-1]
    head_size = model_width // HEADS
    table = head_table(model_width)
    table_low = table.astype(jnp.bfloat16)
    freq = jnp.arange(1, FQ // 4 + 1, dtype=jnp.float32)
    angle_x = 2.0 * math.pi * offsets[0][:, None] * freq[None, :]
    angle_y = 2.0 * math.pi * offsets[1][:, None] * freq[None, :]
    features = jnp.concatenate(
        [jnp.sin(angle_x), jnp.cos(angle_x), jnp.sin(angle_y), jnp.cos(angle_y)], axis=1
    ).astype(jnp.bfloat16)
    probe_query = jnp.dot(features, query_weight, preferred_element_type=jnp.float32).astype(
        jnp.bfloat16
    )
    query_wide = probe_query.astype(jnp.float32)
    score_list = []
    for member in range(9):
        score_list.append(head_sums(table, query_wide * context[:, member].astype(jnp.float32)))
    scores = jnp.stack(score_list) / math.sqrt(head_size)
    weights = jax.nn.softmax(scores, axis=0).astype(jnp.bfloat16)
    mixed = jnp.zeros(probe_query.shape, jnp.float32)
    for member in range(9):
        mixed = mixed + head_spread(weights[member], table_low) * context[:, member].astype(
            jnp.float32
        )
    return jnp.dot(mixed.astype(jnp.bfloat16), head_weight, preferred_element_type=jnp.float32)


def local(
    latents, noise, proc_gain, w_qkv, w_out, w_query, w_head, probe_cell, probe_offset, probe_count
):
    qkv_full, out_full, query_full, head_full = (
        lax.all_gather(w_qkv, ("gx", "pa"), axis=0, tiled=True),
        lax.all_gather(w_out, ("gx", "pa"), axis=0, tiled=True),
        lax.all_gather(w_query, ("gx", "pa"), axis=0, tiled=True),
        lax.all_gather(w_head, ("gx", "pa"), axis=0, tiled=True),
    )
    row_count, col_count, model_width = latents.shape
    latent = latents
    for step in range(STEPS):
        normed = normalize(latent, proc_gain)
        triple = project(normed, qkv_full)
        queries = triple[..., :model_width]
        key_values = extend(triple[..., model_width:])
        attended = neighbour_attention(queries, key_values, row_count, col_count)
        update = jnp.dot(
            attended.reshape(-1, model_width), out_full, preferred_element_type=jnp.float32
        )
        update = update.reshape(row_count, col_count, model_width)
        latent = (
            latent.astype(jnp.float32)
            + update / STEPS
            + NOISE_COEF * noise[step].astype(jnp.float32)
        ).astype(jnp.bfloat16)
    final_ext = extended(latent, ((("gx", "pa"), 0), ("gy", 1)), 1)
    flat_ext = final_ext.reshape(-1, model_width)
    cell_row = probe_cell // col_count
    cell_col = probe_cell % col_count
    index_list = []
    for row_step in range(3):
        for col_step in range(3):
            index_list.append((cell_row + row_step) * (col_count + 2) + cell_col + col_step)
    cell_index = jnp.stack(index_list, axis=1)
    slot_count = probe_cell.shape[0]
    block_size = min(256, slot_count)
    live_count = probe_count[0]

    def decode_at(start):
        rows_index = lax.dynamic_slice_in_dim(cell_index, start, block_size, 0)
        context = jnp.take(flat_ext, rows_index, axis=0)
        offsets = lax.dynamic_slice_in_dim(probe_offset, start, block_size, 1)
        return decode_block(context, offsets, query_full, head_full)

    slots = jnp.arange(slot_count, dtype=jnp.int32)
    starts = jnp.arange(slot_count // block_size, dtype=jnp.int32) * block_size
    values = lax.map(decode_at, starts).reshape(slot_count, CH)
    probe_values = jnp.where((slots < live_count)[None, :], values.T, jnp.zeros((), jnp.float32))
    return (latent, probe_values)


def solution(mesh):
    return jax.shard_map(
        local,
        mesh=mesh,
        in_specs=(
            P(("gx", "pa"), "gy", None),
            P(None, ("gx", "pa"), "gy", None),
            P(),
            P(("gx", "pa"), None),
            P(("gx", "pa"), None),
            P(("gx", "pa"), None),
            P(("gx", "pa"), None),
            P(("gx", "gy", "pa")),
            P(None, ("gx", "gy", "pa")),
            P(("gx", "gy", "pa")),
        ),
        out_specs=(P(("gx", "pa"), "gy", None), P(None, ("gx", "gy", "pa"))),
        check_vma=False,
    )
```

profile of v0, /device:TPU:64, one launch (start us, length us, event | category | flops | bytes accessed | tf_op | source)
XLA Modules:
  0.0 1326.4 jit_solution(11120832807026859498)
XLA Ops:
  11.7 1.7 fusion.166
  13.4 135.1 %all-gather.7.cloned.1.call-done = bf16[128,6,2304]{2,1,0:T(8,128)(2,1)} async-done(((bf16[1,6,2304]{2,1,0:T(8,128)(2,1)}), bf16[128,6,2304]{2,1,0:T(8,128)(2,1)}) %all-gather.7.cloned.1.call-update) | async-done | bytes 3538960 | tf_op jit(solution)/shard_map/all_gather | solution.py:128
  148.5 5.0 reshape.856
  153.5 1.6 convolution_convert_fusion.2
  156.1 8.7 collective-permute-start.1
  164.8 1.9 collective-permute-start
  167.3 99.8 %all-gather.9.cloned.1.call-done = bf16[128,6,768]{2,1,0:T(8,128)(2,1)} async-done(((bf16[1,6,768]{2,1,0:T(8,128)(2,1)}), bf16[128,6,768]{2,1,0:T(8,128)(2,1)}) %all-gather.9.cloned.1.call-update) | async-done | bytes 1179664 | tf_op jit(solution)/shard_map/all_gather | solution.py:129
  267.1 3.2 reshape.863
  273.5 1.9 collective-permute-start.3
  275.4 2.4 collective-permute-start.2
  277.9 1.4 convert_multiply_fusion.70
  281.6 1.7 pad_maximum_fusion
  306.9 1.7 fusion.588
  308.6 1.9 fusion.586
  316.6 6.0 fusion.216
  324.9 7.4 collective-permute-start.5
  332.3 1.9 collective-permute-start.4
  334.8 7.7 collective-permute-done.5
  342.5 12.4 collective-permute-done.4
  355.1 1.9 collective-permute-start.7
  357.0 2.6 collective-permute-start.6
  360.0 3.2 collective-permute-done.6
  388.1 1.7 fusion.582
  395.8 5.4 fusion.168
  402.5 1.9 collective-permute-start.9
  404.5 3.9 collective-permute-start.8
  408.5 8.3 collective-permute-done.8
  416.8 1.9 collective-permute-start.11
  418.7 2.4 collective-permute-start.10
  421.2 368.5 %all-gather.2 = bf16[128,1,768]{2,1,0:T(2,128)(2,1)S(1)} all-gather(bf16[1,1,768]{2,1,0:T(2,128)(2,1)S(1)} %bitcast.1582), channel_id=1, replica_groups=mesh['gx'=32,'gy'=4,'pa'=4] {'gx','pa'}, dimensions={0}, use_global_device_ids=true | all-gather | bytes 198144 | tf_op jit(solution)/shard_map/all_gather | solution.py:130
  789.7 369.0 %all-gather.3 = bf16[128,6,3]{1,2,0:T(4,128)(2,1)S(1)} all-gather(bf16[1,6,3]{1,2,0:T(4,128)(2,1)S(1)} %bitcast.1583), channel_id=1, replica_groups=mesh['gx'=32,'gy'=4,'pa'=4] {'gx','pa'}, dimensions={0}, use_global_device_ids=true | all-gather | bytes 4644 | tf_op jit(solution)/shard_map/all_gather | solution.py:131
  1159.3 159.4 %while.12 = (s32[]{:T(128)}, f32[4,256,3]{1,2,0:T(4,128)S(1)}, s32[4]{0:T(128)S(1)}, f32[2,1024]{1,0:T(2,128)}, bf16[128,768]{1,0:T(8,128)(2,1)S(1)}, /*index=5*...) while((s32[]{:T(128)}, f32[4,256,3]{1,2,0:T(4,128)S(1)}, ...), condition=%wide.region_9.10_spmd, body=%wide.region_6.9_spmd.sunk | while | flops 362281760 | bytes 60195296 | solution.py:171
  1162.3 7.9 gather_fusion
  1170.2 7.2 reshape.872
  1177.5 7.1 copy_select_fusion.2
  1186.1 1.5 fusion.727
  1187.6 1.6 fusion.728
  1189.2 1.6 fusion.729
  1190.7 1.6 fusion.730
  1197.7 1.4 fusion.744
  1202.1 7.9 gather_fusion
  1210.0 7.2 reshape.872
  1217.4 7.1 copy_select_fusion.2
  1226.0 1.5 fusion.727
  1227.5 1.6 fusion.728
  1229.0 1.6 fusion.729
  1230.6 1.6 fusion.730
  1237.6 1.4 fusion.744
  1242.0 7.9 gather_fusion
  1249.9 7.2 reshape.872
  1257.2 7.1 copy_select_fusion.2
  1265.8 1.5 fusion.727
  1267.3 1.6 fusion.728
  1268.9 1.6 fusion.729
  1270.5 1.6 fusion.730
  1277.4 1.4 fusion.744
  1281.9 7.9 gather_fusion
  1289.7 7.2 reshape.872
  1297.1 7.1 copy_select_fusion.2
  1305.7 1.5 fusion.727
  1307.2 1.6 fusion.728
  1308.8 1.6 fusion.729
  1310.3 1.6 fusion.730
  1317.3 1.4 fusion.744
  (411 shorter events, 108.6 us)
Async XLA Ops:
  7.2 141.3 %all-gather.7.cloned.1.call-start = ((), (), s32[]{:S(2)}) async-start(), calls=%async_computation | async-start | bytes 4755456 | tf_op jit(solution)/shard_map/all_gather | solution.py:128
  7.9 259.2 %all-gather.9.cloned.1.call-start = ((), (), s32[]{:S(2)}) async-start(), calls=%async_computation.1 | async-start | bytes 1585152 | tf_op jit(solution)/shard_map/all_gather | solution.py:129
  155.1 9.7 copy-start.1
  156.1 116.3 %collective-permute-start.1 = (bf16[3,32,1536]{2,1,0:T(8,128)(2,1)}, bf16[3,32,1536]{2,1,0:T(8,128)(2,1)}, u32[]{:S(2)}, u32[]{:S(2)}) collective-permute-start(bf16[3,32,1536]{2,1,0:T(8,128)(2,1)} %get-tuple-element.384), channel_id=1, source_target_pairs={{1,0},{2,1},{3,2},{16,3},{17,16},{18,17},{19,18},{32,19},{33,32},{... | collective-permute-start | bytes 884744 | tf_op jit(solution)/shard_map/ppermute | solution.py:25
  164.8 107.6 %collective-permute-start = (bf16[3,32,1536]{2,1,0:T(8,128)(2,1)}, bf16[3,32,1536]{2,1,0:T(8,128)(2,1)}, u32[]{:S(2)}, u32[]{:S(2)}) collective-permute-start(bf16[3,32,1536]{2,1,0:T(8,128)(2,1)} %get-tuple-element.383), channel_id=1, source_target_pairs={{0,1},{1,2},{2,3},{3,16},{16,17},{17,18},{18,19},{19,32},{32,33},{... | collective-permute-start | bytes 884744 | tf_op jit(solution)/shard_map/ppermute | solution.py:22
  270.3 7.5 copy-start.2
  273.5 7.0 collective-permute-start.3
  275.4 6.2 collective-permute-start.2
  316.6 6.1 copy-start.3
  316.6 6.1 copy-start.5
  316.6 7.5 copy-start.6
  324.9 17.7 %collective-permute-start.5 = (bf16[3,32,1536]{2,1,0:T(8,128)(2,1)S(1)}, bf16[3,32,1536]{2,1,0:T(8,128)(2,1)S(1)}, u32[]{:S(2)}, u32[]{:S(2)}) collective-permute-start(bf16[3,32,1536]{2,1,0:T(8,128)(2,1)S(1)} %get-tuple-element.378), channel_id=1, source_target_pairs={{1,0},{2,1},{3,2},{16,3},{17,16},{18,17},{19,18},{32,19},{33,32},{... | collective-permute-start | bytes 884744 | tf_op jit(solution)/shard_map/ppermute | solution.py:25
  332.3 22.7 %collective-permute-start.4 = (bf16[3,32,1536]{2,1,0:T(8,128)(2,1)S(1)}, bf16[3,32,1536]{2,1,0:T(8,128)(2,1)S(1)}, u32[]{:S(2)}, u32[]{:S(2)}) collective-permute-start(bf16[3,32,1536]{2,1,0:T(8,128)(2,1)S(1)} %get-tuple-element.377), channel_id=1, source_target_pairs={{0,1},{1,2},{2,3},{3,16},{16,17},{17,18},{18,19},{19,32},{32,33},{... | collective-permute-start | bytes 884744 | tf_op jit(solution)/shard_map/ppermute | solution.py:22
  355.1 5.0 collective-permute-start.7
  357.0 6.2 collective-permute-start.6
  401.2 20.0 %copy-start.11 = (bf16[1,768]{1,0:T(2,128)(2,1)S(1)}, bf16[1,768]{1,0:T(2,128)(2,1)}, u32[]{:S(2)}) copy-start(bf16[1,768]{1,0:T(2,128)(2,1)} %param.17) | copy-start | bytes 4612
  401.2 388.6 %copy-start.12 = (bf16[6,3]{0,1:T(4,128)(2,1)S(1)}, bf16[6,3]{0,1:T(4,128)(2,1)}, u32[]{:S(2)}) copy-start(bf16[6,3]{0,1:T(4,128)(2,1)} %param.18) | copy-start | bytes 112
  401.2 757.7 %copy-start.7 = (s32[1024]{0:T(1024)S(1)}, s32[1024]{0:T(1024)}, u32[]{:S(2)}) copy-start(s32[1024]{0:T(1024)} %get-tuple-element.153) | copy-start | bytes 12292
  401.2 757.7 %copy-start.8 = (s32[1024]{0:T(1024)S(1)}, s32[1024]{0:T(1024)}, u32[]{:S(2)}) copy-start(s32[1024]{0:T(1024)} %get-tuple-element.395) | copy-start | bytes 12292
  401.2 757.7 %copy-start.9 = (s32[1024]{0:T(1024)S(1)}, s32[1024]{0:T(1024)}, u32[]{:S(2)}) copy-start(s32[1024]{0:T(1024)} %get-tuple-element.397) | copy-start | bytes 12292
  401.2 757.7 %copy-start.10 = (s32[1024]{0:T(1024)S(1)}, s32[1024]{0:T(1024)}, u32[]{:S(2)}) copy-start(s32[1024]{0:T(1024)} %broadcast_add_fusion.5) | copy-start | bytes 12292
  402.5 756.8 %copy-start.4 = (bf16[4,32,768]{2,1,0:T(8,128)(2,1)}, bf16[4,32,768]{2,1,0:T(8,128)(2,1)S(1)}, u32[]{:S(2)}) copy-start(bf16[4,32,768]{2,1,0:T(8,128)(2,1)S(1)} %fusion.63) | copy-start | bytes 589828
  402.5 6.0 collective-permute-start.9
  404.5 12.3 collective-permute-start.8
  416.8 742.2 %collective-permute-start.11 = (bf16[6,1,768]{2,1,0:T(2,128)(2,1)S(1)}, bf16[6,1,768]{2,1,0:T(2,128)(2,1)S(1)}, u32[]{:S(2)}, u32[]{:S(2)}) collective-permute-start(bf16[6,1,768]{2,1,0:T(2,128)(2,1)S(1)} %get-tuple-element.392), channel_id=1, source_target_pairs={{4,0},{8,4},{12,8},{0,12},{5,1},{9,5},{13,9},{1,13},{6,2},{10,6},{... | collective-permute-start | bytes 27656 | tf_op jit(solution)/shard_map/ppermute | solution.py:25
  418.7 740.3 %collective-permute-start.10 = (bf16[6,1,768]{2,1,0:T(2,128)(2,1)S(1)}, bf16[6,1,768]{2,1,0:T(2,128)(2,1)S(1)}, u32[]{:S(2)}, u32[]{:S(2)}) collective-permute-start(bf16[6,1,768]{2,1,0:T(2,128)(2,1)S(1)} %get-tuple-element.391), channel_id=1, source_target_pairs={{0,4},{4,8},{8,12},{12,0},{1,5},{5,9},{9,13},{13,1},{2,6},{6,10},{... | collective-permute-start | bytes 27656 | tf_op jit(solution)/shard_map/ppermute | solution.py:22
  1159.3 159.5 %copy-start.13 = (pred[1024]{0:T(1024)(128)(4,1)S(1)}, pred[1024]{0:T(1024)(128)(4,1)}, u32[]{:S(2)}) copy-start(pred[1024]{0:T(1024)(128)(4,1)} %iota_compare_fusion.217) | copy-start | bytes 3076
  1184.6 7.8 copy-start
  1224.4 7.8 copy-start
  1264.3 7.8 copy-start
  1304.2 7.8 copy-start
Sparse Core Ops, SparseCore 0:
  12.4 135.9 all-gather.6
  152.8 114.3 all-gather.8
where the time goes:
time: 1340 us; the launch traced here: 1330 us
  blocking collectives  738 us (55%)
  waiting for transfers between devices  269 us (20%)
  matrix products  122 us (9%)
  local copies, waits for them, and re-layouts  83.2 us (6%)
  other arithmetic  50.9 us (4%)
  starting transfers between devices  39.1 us (3%)
  between operations  16.1 us (1%)
    all_gather x1, blocking collectives, local(): lax.all_gather(w_head, ('gx', 'pa'), axis=0, tiled=True)  369 us
    all_gather x1, blocking collectives, local(): lax.all_gather(w_query, ('gx', 'pa'), axis=0, tiled=True)  369 us
    all_gather x1, waiting for transfers between devices, local(): lax.all_gather(w_qkv, ('gx', 'pa'), axis=0, tiled=True)  135 us
    all_gather x1, waiting for transfers between devices, local(): lax.all_gather(w_out, ('gx', 'pa'), axis=0, tiled=True)  99.8 us
    dot_general x134, matrix products, head_sums(): lax.dot_general(table, product, (((1,), (1,)), ((), ())), precision=lax.P...  66.4 us
    gather x8, local copies, waits for them, and re-layouts, decode_at(): context = jnp.take(flat_ext, rows_index, axis=0)  60.4 us
    dot_general x130, matrix products, head_spread(): lax.dot_general(weight_rows, table_low, (((0,), (0,)), ((), ())), preferr...  44.2 us
    select_n x8, other arithmetic, decode_at(): context = jnp.take(flat_ext, rows_index, axis=0)  28.3 us
  transfers between devices with their start and end apart: 14, of which 8 were waited for; matrix products, arithmetic and copies ran while one was open for 2% of the time, Pallas kernels for 0%

commit v1 on v0

--- a/solution.py
+++ b/solution.py
@@ -127,7 +127,10 @@
     qkv_full, out_full, query_full, head_full = (
         lax.all_gather(w_qkv, ("gx", "pa"), axis=0, tiled=True),
         lax.all_gather(w_out, ("gx", "pa"), axis=0, tiled=True),
-        lax.all_gather(w_query, ("gx", "pa"), axis=0, tiled=True),
+        jnp.concatenate(
+            lax.all_to_all(jnp.stack([w_query] * lax.axis_size(("gx", "pa"))), ("gx", "pa"), 0, 0),
+            axis=0,
+        ),
         lax.all_gather(w_head, ("gx", "pa"), axis=0, tiled=True),
     )
     row_count, col_count, model_width = latents.shape

time: 1340 us -> 966 us (0.72)
  the two profiles are of different devices: /device:TPU:64 before, /device:TPU:2 now
where the time goes in v1:
time: 966 us; the launch traced here: 959 us
  blocking collectives  373 us (39%)
  waiting for transfers between devices  237 us (25%)
  matrix products  122 us (13%)
  local copies, waits for them, and re-layouts  86.2 us (9%)
  starting transfers between devices  63.5 us (7%)
  other arithmetic  52.8 us (5%)
  between operations  16.3 us (2%)
    all_gather x1, blocking collectives, local(): lax.all_gather(w_head, ('gx', 'pa'), axis=0, tiled=True)  373 us
    all_gather x1, waiting for transfers between devices, local(): lax.all_gather(w_qkv, ('gx', 'pa'), axis=0, tiled=True)  116 us
    all_gather x1, waiting for transfers between devices, local(): lax.all_gather(w_out, ('gx', 'pa'), axis=0, tiled=True)  103 us
    dot_general x134, matrix products, head_sums(): lax.dot_general(table, product, (((1,), (1,)), ((), ())), precision=lax.P...  66.4 us
    gather x8, local copies, waits for them, and re-layouts, decode_at(): context = jnp.take(flat_ext, rows_index, axis=0)  60.4 us
    dot_general x130, matrix products, head_spread(): lax.dot_general(weight_rows, table_low, (((0,), (0,)), ((), ())), preferr...  43.7 us
    select_n x8, other arithmetic, decode_at(): context = jnp.take(flat_ext, rows_index, axis=0)  28.4 us
    ppermute x6, starting transfers between devices, extended(): lax.ppermute(lax.slice_in_dim(block, 0, width, axis=dim), axis, backward)  27.1 us
  transfers between devices with their start and end apart: 15, of which 7 were waited for; matrix products, arithmetic and copies ran while one was open for 11% of the time, Pallas kernels for 0%

profile of v1, /device:TPU:2, one launch (start us, length us, event | category | flops | bytes accessed | tf_op | source)
XLA Modules:
  0.0 959.2 jit_solution(15514507087944280490)
XLA Ops:
  10.1 1.8 reduce.1
  12.6 20.3 %all-to-all-start = ((bf16[128,2,384]{2,1,0:T(2,128)(2,1)}), bf16[128,2,384]{2,1,0:T(2,128)(2,1)}, u32[]{:S(2)}, u32[]{:S(2)}) async-start(bf16[128,2,384]{2,1,0:T(2,128)(2,1)} %reshape.871), calls=%async_computation | async-start | bytes 393216 | tf_op jit(solution)/shard_map/all_to_all | solution.py:131
  34.0 1.7 fusion.166
  35.7 115.9 %all-gather.6.cloned.1.call-done = bf16[128,6,2304]{2,1,0:T(8,128)(2,1)} async-done(((bf16[1,6,2304]{2,1,0:T(8,128)(2,1)}), bf16[128,6,2304]{2,1,0:T(8,128)(2,1)}) %all-gather.6.cloned.1.call-update) | async-done | bytes 3538960 | tf_op jit(solution)/shard_map/all_gather | solution.py:128
  151.7 5.0 reshape.863
  156.7 1.6 convolution_convert_fusion.2
  159.3 2.5 collective-permute-start.1
  161.7 3.4 collective-permute-start
  165.8 102.8 %all-gather.8.cloned.1.call-done = bf16[128,6,768]{2,1,0:T(8,128)(2,1)} async-done(((bf16[1,6,768]{2,1,0:T(8,128)(2,1)}), bf16[128,6,768]{2,1,0:T(8,128)(2,1)}) %all-gather.8.cloned.1.call-update) | async-done | bytes 1179664 | tf_op jit(solution)/shard_map/all_gather | solution.py:129
  268.6 3.2 reshape.868
  274.9 1.9 collective-permute-start.3
  276.9 2.6 collective-permute-start.2
  283.1 1.6 pad_maximum_fusion
  308.3 1.7 fusion.588
  310.1 1.9 fusion.586
  318.0 6.0 fusion.216
  326.2 2.5 collective-permute-start.5
  328.7 3.4 collective-permute-start.4
  334.0 2.6 collective-permute-done.5
  336.5 6.1 collective-permute-done.4
  342.8 2.6 collective-permute-start.7
  345.4 2.4 collective-permute-start.6
  348.2 3.4 collective-permute-done.6
  376.2 1.7 fusion.582
  383.9 5.3 fusion.168
  390.6 15.7 %collective-permute-start.9 = (bf16[1,32,768]{2,1,0:T(8,128)(2,1)S(1)}, bf16[1,32,768]{2,1,0:T(8,128)(2,1)S(1)}, u32[]{:S(2)}, u32[]{:S(2)}) collective-permute-start(bf16[1,32,768]{2,1,0:T(8,128)(2,1)S(1)} %get-tuple-element.394), channel_id=1, source_target_pairs={{1,0},{2,1},{3,2},{16,3},{17,16},{18,17},{19,18},{32,19},{33,32},{... | collective-permute-start | bytes 147464 | tf_op jit(solution)/shard_map/ppermute | solution.py:25
  406.3 1.9 collective-permute-start.8
  408.2 4.0 collective-permute-done.8
  412.3 1.9 collective-permute-start.11
  414.2 2.4 collective-permute-start.10
  416.7 373.1 %all-gather.2 = bf16[128,6,3]{1,2,0:T(4,128)(2,1)S(1)} all-gather(bf16[1,6,3]{1,2,0:T(4,128)(2,1)S(1)} %bitcast.1581), channel_id=1, replica_groups=mesh['gx'=32,'gy'=4,'pa'=4] {'gx','pa'}, dimensions={0}, use_global_device_ids=true | all-gather | bytes 4644 | tf_op jit(solution)/shard_map/all_gather | solution.py:134
  790.1 1.6 reshape.872
  791.9 159.6 %while.12 = (s32[]{:T(128)}, f32[4,256,3]{1,2,0:T(4,128)S(1)}, s32[4]{0:T(128)S(1)}, f32[2,1024]{1,0:T(2,128)}, bf16[128,768]{1,0:T(8,128)(2,1)S(1)}, /*index=5*...) while((s32[]{:T(128)}, f32[4,256,3]{1,2,0:T(4,128)S(1)}, ...), condition=%wide.region_9.10_spmd, body=%wide.region_6.9_spmd.sunk | while | flops 362281760 | bytes 60195296 | solution.py:174
  794.9 7.9 gather_fusion
  802.8 7.2 reshape.880
  810.2 7.1 copy_select_fusion.2
  818.8 1.5 fusion.727
  820.3 1.6 fusion.728
  821.8 1.6 fusion.729
  823.4 1.6 fusion.730
  830.4 1.4 fusion.744
  834.8 7.9 gather_fusion
  842.7 7.2 reshape.880
  850.0 7.1 copy_select_fusion.2
  858.7 1.5 fusion.727
  860.2 1.6 fusion.728
  861.7 1.6 fusion.729
  863.3 1.6 fusion.730
  870.3 1.4 fusion.744
  874.7 7.9 gather_fusion
  882.6 7.2 reshape.880
  889.9 7.1 copy_select_fusion.2
  898.6 1.5 fusion.727
  900.1 1.6 fusion.728
  901.6 1.6 fusion.729
  903.2 1.6 fusion.730
  910.2 1.4 fusion.744
  914.6 7.9 gather_fusion
  922.5 7.2 reshape.880
  929.8 7.1 copy_select_fusion.2
  938.5 1.5 fusion.727
  940.0 1.6 fusion.728
  941.5 1.6 fusion.729
  943.1 1.6 fusion.730
  (420 shorter events, 112.3 us)
Async XLA Ops:
  7.2 144.5 %all-gather.6.cloned.1.call-start = ((), (), s32[]{:S(2)}) async-start(), calls=%async_computation.1 | async-start | bytes 4755456 | tf_op jit(solution)/shard_map/all_gather | solution.py:128
  7.9 260.7 %all-gather.8.cloned.1.call-start = ((), (), s32[]{:S(2)}) async-start(), calls=%async_computation.2 | async-start | bytes 1585152 | tf_op jit(solution)/shard_map/all_gather | solution.py:129
  12.6 777.5 %all-to-all-start = ((bf16[128,2,384]{2,1,0:T(2,128)(2,1)}), bf16[128,2,384]{2,1,0:T(2,128)(2,1)}, u32[]{:S(2)}, u32[]{:S(2)}) async-start(bf16[128,2,384]{2,1,0:T(2,128)(2,1)} %reshape.871), calls=%async_computation | async-start | bytes 393216 | tf_op jit(solution)/shard_map/all_to_all | solution.py:131
  156.7 8.4 copy-start.13
  158.3 3.4 copy-start.1
  159.3 114.6 %collective-permute-start.1 = (bf16[3,32,1536]{2,1,0:T(8,128)(2,1)}, bf16[3,32,1536]{2,1,0:T(8,128)(2,1)}, u32[]{:S(2)}, u32[]{:S(2)}) collective-permute-start(bf16[3,32,1536]{2,1,0:T(8,128)(2,1)} %get-tuple-element.384), channel_id=1, source_target_pairs={{1,0},{2,1},{3,2},{16,3},{17,16},{18,17},{19,18},{32,19},{33,32},{... | collective-permute-start | bytes 884744 | tf_op jit(solution)/shard_map/ppermute | solution.py:25
  161.7 112.1 %collective-permute-start = (bf16[3,32,1536]{2,1,0:T(8,128)(2,1)}, bf16[3,32,1536]{2,1,0:T(8,128)(2,1)}, u32[]{:S(2)}, u32[]{:S(2)}) collective-permute-start(bf16[3,32,1536]{2,1,0:T(8,128)(2,1)} %get-tuple-element.383), channel_id=1, source_target_pairs={{0,1},{1,2},{2,3},{3,16},{16,17},{17,18},{18,19},{19,32},{32,33},{... | collective-permute-start | bytes 884744 | tf_op jit(solution)/shard_map/ppermute | solution.py:22
  271.8 7.7 copy-start.2
  274.9 7.2 collective-permute-start.3
  276.9 6.2 collective-permute-start.2
  318.0 6.0 copy-start.3
  318.0 6.0 copy-start.5
  318.0 7.4 copy-start.6
  326.2 10.3 %collective-permute-start.5 = (bf16[3,32,1536]{2,1,0:T(8,128)(2,1)S(1)}, bf16[3,32,1536]{2,1,0:T(8,128)(2,1)S(1)}, u32[]{:S(2)}, u32[]{:S(2)}) collective-permute-start(bf16[3,32,1536]{2,1,0:T(8,128)(2,1)S(1)} %get-tuple-element.378), channel_id=1, source_target_pairs={{1,0},{2,1},{3,2},{16,3},{17,16},{18,17},{19,18},{32,19},{33,32},{... | collective-permute-start | bytes 884744 | tf_op jit(solution)/shard_map/ppermute | solution.py:25
  328.7 14.0 %collective-permute-start.4 = (bf16[3,32,1536]{2,1,0:T(8,128)(2,1)S(1)}, bf16[3,32,1536]{2,1,0:T(8,128)(2,1)S(1)}, u32[]{:S(2)}, u32[]{:S(2)}) collective-permute-start(bf16[3,32,1536]{2,1,0:T(8,128)(2,1)S(1)} %get-tuple-element.377), channel_id=1, source_target_pairs={{0,1},{1,2},{2,3},{3,16},{16,17},{17,18},{18,19},{19,32},{32,33},{... | collective-permute-start | bytes 884744 | tf_op jit(solution)/shard_map/ppermute | solution.py:22
  342.8 5.4 collective-permute-start.7
  345.4 6.2 collective-permute-start.6
  389.2 27.4 %copy-start.14 = (bf16[6,3]{0,1:T(4,128)(2,1)S(1)}, bf16[6,3]{0,1:T(4,128)(2,1)}, u32[]{:S(2)}) copy-start(bf16[6,3]{0,1:T(4,128)(2,1)} %param.18) | copy-start | bytes 112
  389.2 400.7 %copy-start.7 = (s32[1024]{0:T(1024)S(1)}, s32[1024]{0:T(1024)}, u32[]{:S(2)}) copy-start(s32[1024]{0:T(1024)} %get-tuple-element.153) | copy-start | bytes 12292
  389.2 400.7 %copy-start.8 = (s32[1024]{0:T(1024)S(1)}, s32[1024]{0:T(1024)}, u32[]{:S(2)}) copy-start(s32[1024]{0:T(1024)} %get-tuple-element.395) | copy-start | bytes 12292
  389.2 400.7 %copy-start.9 = (s32[1024]{0:T(1024)S(1)}, s32[1024]{0:T(1024)}, u32[]{:S(2)}) copy-start(s32[1024]{0:T(1024)} %get-tuple-element.397) | copy-start | bytes 12292
  389.2 400.7 %copy-start.10 = (s32[1024]{0:T(1024)S(1)}, s32[1024]{0:T(1024)}, u32[]{:S(2)}) copy-start(s32[1024]{0:T(1024)} %broadcast_add_fusion.5) | copy-start | bytes 12292
  389.3 400.7 %copy-start.11 = (s32[1024]{0:T(1024)S(1)}, s32[1024]{0:T(1024)}, u32[]{:S(2)}) copy-start(s32[1024]{0:T(1024)} %get-tuple-element.403) | copy-start | bytes 12292
  389.3 400.7 %copy-start.12 = (s32[1024]{0:T(1024)S(1)}, s32[1024]{0:T(1024)}, u32[]{:S(2)}) copy-start(s32[1024]{0:T(1024)} %get-tuple-element.404) | copy-start | bytes 12292
  390.6 401.4 %copy-start.4 = (bf16[4,32,768]{2,1,0:T(8,128)(2,1)}, bf16[4,32,768]{2,1,0:T(8,128)(2,1)S(1)}, u32[]{:S(2)}) copy-start(bf16[4,32,768]{2,1,0:T(8,128)(2,1)S(1)} %fusion.63) | copy-start | bytes 589828
  390.6 17.6 %collective-permute-start.9 = (bf16[1,32,768]{2,1,0:T(8,128)(2,1)S(1)}, bf16[1,32,768]{2,1,0:T(8,128)(2,1)S(1)}, u32[]{:S(2)}, u32[]{:S(2)}) collective-permute-start(bf16[1,32,768]{2,1,0:T(8,128)(2,1)S(1)} %get-tuple-element.394), channel_id=1, source_target_pairs={{1,0},{2,1},{3,2},{16,3},{17,16},{18,17},{19,18},{32,19},{33,32},{... | collective-permute-start | bytes 147464 | tf_op jit(solution)/shard_map/ppermute | solution.py:25
  406.3 6.0 collective-permute-start.8
  412.3 379.4 %collective-permute-start.11 = (bf16[6,1,768]{2,1,0:T(2,128)(2,1)S(1)}, bf16[6,1,768]{2,1,0:T(2,128)(2,1)S(1)}, u32[]{:S(2)}, u32[]{:S(2)}) collective-permute-start(bf16[6,1,768]{2,1,0:T(2,128)(2,1)S(1)} %get-tuple-element.392), channel_id=1, source_target_pairs={{4,0},{8,4},{12,8},{0,12},{5,1},{9,5},{13,9},{1,13},{6,2},{10,6},{... | collective-permute-start | bytes 27656 | tf_op jit(solution)/shard_map/ppermute | solution.py:25
  414.2 377.5 %collective-permute-start.10 = (bf16[6,1,768]{2,1,0:T(2,128)(2,1)S(1)}, bf16[6,1,768]{2,1,0:T(2,128)(2,1)S(1)}, u32[]{:S(2)}, u32[]{:S(2)}) collective-permute-start(bf16[6,1,768]{2,1,0:T(2,128)(2,1)S(1)} %get-tuple-element.391), channel_id=1, source_target_pairs={{0,4},{4,8},{8,12},{12,0},{1,5},{5,9},{9,13},{13,1},{2,6},{6,10},{... | collective-permute-start | bytes 27656 | tf_op jit(solution)/shard_map/ppermute | solution.py:22
  817.2 7.8 copy-start
  857.1 7.8 copy-start
  897.0 7.8 copy-start
  936.9 7.8 copy-start
Sparse Core Ops, SparseCore 0:
  12.4 139.1 all-gather.5
  156.0 112.5 all-gather.7
